TPU v7x, 32 devices: a whole 2x2x4 slice. The times are simulated.
32 devices in a mesh: frames: 2 (over y), row: 4 (over x, core), col: 4 (over z).
Axes of the slice: x: 2, y: 2, z: 4, core: 2. Of those that a mesh axis runs over, the one named last changes fastest.
Arguments:
- mask_pixels: int32 [2048, 2048], P(('frames', 'row'), 'col'), parts along dimension 0, may hold values 0 or 1
- across_taps: bfloat16 [12, 2, 33], replicated, may hold values from -1 to 1
- down_taps: bfloat16 [12, 2, 33], replicated, may hold values from -1 to 1
- kernel_weights: float32 [12], replicated, may hold values from 0.05 to 0.5
- library: bfloat16 [32, 64, 128], P('col'), may hold values from 0 to 4
- cell_ids: int32 [8, 4, 8], P(('frames', 'row'), 'col'), parts along dimension 0, may hold values from 0 to 31, as said below
- cell_slots: int32 [8, 4, 8], P(('frames', 'row'), 'col'), parts along dimension 0, may hold values from 0 to 15, as said below
- cell_count: int32 [8, 4], P(('frames', 'row'), 'col'), parts along dimension 0, may hold values from 2 to 8
Outputs:
- resist: float32 [2048, 2048], P(('frames', 'row'), 'col'), parts along dimension 0
There are 2 independent parts, one for each index of `frames`. A program takes and returns all parts, laid end to end along the dimension named above; an argument that names none is the same for every part. Nothing has to cross between parts.
Inputs may be any that keep to these rules, and one draw needn't show every extreme that they name: `cell_ids`: among the 8 entries of a tile's list, at most 2 name cells of one block of 8 consecutive ids (k * 8 to k * 8 + 7), and the first two entries name cells of one such block. `cell_slots`: the slots of a tile's list are distinct.
All inputs are finite; a program needn't handle non-finite values. No bound on the sum of `mask_pixels` on one device may be relied on, other than what follows from the above.
Results may differ from a plain program's by a relative error of at most 0.00045.
Values may be sent and summed in bfloat16 or wider, within the bound.
A program may use at most 64 MiB of HBM per device.

v0:
```python
import jax
import jax.numpy as jnp
from jax import lax
from jax.sharding import PartitionSpec as P

BLUR_HALF = 8


BLUR_SIGMA = 4.0


def extended_2(x, sides, width):
    for axis, dim in sides:
        count, length = (lax.axis_size(axis), x.shape[dim])
        up = [(i, (i + 1) % count) for i in range(count - 1)]
        down = [(j, i) for i, j in up]
        last = lax.slice_in_dim(x, length - width, length, axis=dim)
        initial = lax.slice_in_dim(x, 0, width, axis=dim)
        before = lax.ppermute(last, axis, up)
        after = lax.ppermute(initial, axis, down)
        x = jnp.concatenate([before, x, after], axis=dim)
    return x


def band_matrix(tap_values, half_width):
    window = 128 + 2 * half_width
    grid_shape = (window, 128, 2 * half_width + 1)
    in_index = lax.broadcasted_iota(jnp.int32, grid_shape, 0)
    out_index = lax.broadcasted_iota(jnp.int32, grid_shape, 1)
    lag_index = lax.broadcasted_iota(jnp.int32, grid_shape, 2)
    picker = (in_index - out_index == lag_index).astype(tap_values.dtype)
    return jnp.einsum(
        "...t,ijt->...ij",
        tap_values,
        picker,
        preferred_element_type=jnp.float32,
        precision=lax.Precision.HIGHEST,
    )


def blur_taps(half_width):
    offsets = (
        lax.broadcasted_iota(jnp.int32, (2 * half_width + 1,), 0).astype(jnp.float32) - half_width
    )
    weights = jnp.exp(-offsets * offsets / (2.0 * BLUR_SIGMA * BLUR_SIGMA))
    return weights / jnp.sum(weights)


def windows_last(padded, half_width):
    length = padded.shape[-1] - 2 * half_width
    blocks = length // 128
    pad_spec = [(0, 0)] * (padded.ndim - 1) + [(0, 128 - 2 * half_width)]
    spread = jnp.pad(padded, pad_spec).reshape(padded.shape[:-1] + (blocks + 1, 128))
    return jnp.concatenate([spread[..., :blocks, :], spread[..., 1:, : 2 * half_width]], axis=-1)


def windows_rows(padded, half_width):
    length = padded.shape[-2] - 2 * half_width
    blocks = length // 128
    pad_spec = [(0, 0)] * (padded.ndim - 2) + [(0, 128 - 2 * half_width), (0, 0)]
    spread = jnp.pad(padded, pad_spec).reshape(
        padded.shape[:-2] + (blocks + 1, 128, padded.shape[-1])
    )
    return jnp.concatenate(
        [spread[..., :blocks, :, :], spread[..., 1:, : 2 * half_width, :]], axis=-2
    )


def blur_straight(extended, blur_mat, half_width):
    sideways = jnp.einsum(
        "rbi,ij->rbj", windows_last(extended, half_width), blur_mat, precision=lax.Precision.HIGHEST
    )
    sideways = sideways.reshape(extended.shape[0], -1)
    downward = jnp.einsum(
        "biw,ij->bjw", windows_rows(sideways, half_width), blur_mat, precision=lax.Precision.HIGHEST
    )
    return downward.reshape(-1, sideways.shape[1])


def place_cells(library, cell_ids, cell_slots, cell_count, tile_rows, tile_cols, out_spec):
    cell_rows, cell_cols = (library.shape[1], library.shape[2])
    slot_rows = tile_rows // cell_rows
    slot_cols = tile_cols // cell_cols
    entries = cell_ids.shape[-1]
    ids_flat = cell_ids.reshape(entries)
    entry_iota = lax.broadcasted_iota(jnp.int32, (entries,), 0)
    is_live = entry_iota < cell_count.reshape(())
    slot_hit = (
        cell_slots.reshape(entries, 1)
        == lax.broadcasted_iota(jnp.int32, (1, slot_rows * slot_cols), 1)
    ) & is_live[:, None]
    slot_hit = slot_hit.astype(jnp.float32)
    sizes_by_letter = {"a": slot_rows, "p": cell_rows, "b": slot_cols, "q": cell_cols}
    empty_sum = jnp.zeros(tuple((sizes_by_letter[letter] for letter in out_spec)), jnp.float32)
    shard_cells = lax.all_gather(library, "col", axis=0, tiled=True)
    count_here = shard_cells.shape[0]
    id_match = (ids_flat[:, None] == lax.broadcasted_iota(jnp.int32, (1, count_here), 1)).astype(
        jnp.float32
    )
    place_table = (
        jnp.dot(slot_hit.T, id_match).reshape(slot_rows, slot_cols, count_here).astype(jnp.bfloat16)
    )
    return empty_sum + jnp.einsum(
        "abk,kpq->" + out_spec, place_table, shard_cells, preferred_element_type=jnp.float32
    )


def on_device(
    mask_pixels, across_taps, down_taps, kernel_weights, library, cell_ids, cell_slots, cell_count
):
    tile_rows, tile_cols = mask_pixels.shape
    half_width = (across_taps.shape[-1] - 1) // 2
    pixels = mask_pixels.astype(jnp.bfloat16)
    padded_mask = extended_2(pixels, (("col", 1),), half_width)
    first_mats = band_matrix(across_taps, half_width).astype(jnp.bfloat16)
    second_mats = band_matrix(down_taps, half_width).astype(jnp.bfloat16)
    blur_mat = band_matrix(blur_taps(BLUR_HALF), BLUR_HALF)
    tall_mask = extended_2(padded_mask, (("row", 0),), half_width)
    tall_windows = windows_last(tall_mask, half_width)
    tall_rows = tile_rows + 2 * half_width

    def kernel_step(running, inputs):
        first_mat, second_mat, weight = inputs
        pass_one = jnp.einsum(
            "rbi,pij->prbj", tall_windows, first_mat, preferred_element_type=jnp.float32
        )
        pass_one = pass_one.reshape(2, tall_rows, tile_cols).astype(jnp.bfloat16)
        pass_two = jnp.einsum(
            "pbiw,pij->pbjw",
            windows_rows(pass_one, half_width),
            second_mat,
            preferred_element_type=jnp.float32,
        )
        pass_two = pass_two.reshape(2, tile_rows, tile_cols)
        return (running + weight * jnp.sum(pass_two * pass_two, axis=0), None)

    start_total = jnp.zeros((tile_rows, tile_cols), jnp.float32)
    flat_image = lax.scan(kernel_step, start_total, (first_mats, second_mats, kernel_weights))[0]
    placed = place_cells(library, cell_ids, cell_slots, cell_count, tile_rows, tile_cols, "apbq")
    intensity = flat_image + placed.reshape(tile_rows, tile_cols)
    extended = extended_2(
        intensity.astype(jnp.bfloat16), (("row", 0), ("col", 1)), BLUR_HALF
    ).astype(intensity.dtype)
    return blur_straight(extended, blur_mat, BLUR_HALF)


def solution(mesh):
    placed = (
        P(("frames", "row"), "col"),
        P(),
        P(),
        P(),
        P("col", None, None),
        P(("frames", "row"), "col", None),
        P(("frames", "row"), "col", None),
        P(("frames", "row"), "col"),
    )
    return jax.shard_map(
        on_device,
        mesh=mesh,
        in_specs=placed,
        out_specs=P(("frames", "row"), "col"),
        check_vma=False,
    )
```

profile of v0, /device:TPU:0, one launch (start us, length us, event | category | flops | bytes accessed | tf_op | source)
XLA Modules:
  0.0 97.8 jit_solution(8133458689836300485)
XLA Ops:
  0.0 1.1 %convert_element_type.62 = bf16[256,512]{1,0:T(8,128)(2,1)S(1)} convert(s32[256,512]{1,0:T(8,128)} %param.10) | non-fusion elementwise | flops 131072 | bytes 786432 | tf_op jit(solution)/shard_map/convert_element_type | solution.py:113
  1.2 4.9 %collective-permute-start = (bf16[256,16]{1,0:T(8,128)(2,1)S(1)}, bf16[256,16]{1,0:T(8,128)(2,1)S(1)}, u32[]{:S(2)}, u32[]{:S(2)}) collective-permute-start(bf16[256,16]{1,0:T(8,128)(2,1)S(1)} %get-tuple-element.140), channel_id=1, source_target_pairs={{0,1},{1,2},{2,3},{4,5},{5,6},{6,7},{8,9},{9,10},{10,11},{12,13},{... | collective-permute-start | bytes 24584 | tf_op jit(solution)/shard_map/ppermute | solution.py:19
  6.1 1.3 %collective-permute-start.1 = (bf16[256,16]{1,0:T(8,128)(2,1)S(1)}, bf16[256,16]{1,0:T(8,128)(2,1)S(1)}, u32[]{:S(2)}, u32[]{:S(2)}) collective-permute-start(bf16[256,16]{1,0:T(8,128)(2,1)S(1)} %get-tuple-element.141), channel_id=1, source_target_pairs={{1,0},{2,1},{3,2},{5,4},{6,5},{7,6},{9,8},{10,9},{11,10},{13,12},{... | collective-permute-start | bytes 24584 | tf_op jit(solution)/shard_map/ppermute | solution.py:20
  7.4 1.4 %fusion.29 = bf16[12,2,160,128]{3,0,1,2:T(8,128)(2,1)S(1)} fusion(bf16[12,2,33]{2,1,0:T(2,128)(2,1)} %param.12), kind=kOutput, calls=%fused_computation.27 | convolution fusion | flops 34283520 | bytes 984624 | tf_op jit(solution)/shard_map/...t,ijt->...ij/dot_general | solution.py:32
  8.9 1.8 %fusion.26 = bf16[12,2,160,128]{3,0,1,2:T(8,128)(2,1)} fusion(bf16[12,2,33]{2,1,0:T(2,128)(2,1)S(1)} %copy-done.2), kind=kOutput, calls=%fused_computation.26 | convolution fusion | flops 34283520 | bytes 984624 | tf_op jit(solution)/shard_map/...t,ijt->...ij/dot_general | solution.py:32
  11.8 16.1 %all_gather.3 = bf16[32,64,128]{2,0,1:T(8,128)(2,1)S(1)} all-gather(bf16[8,64,128]{2,0,1:T(8,128)(2,1)S(1)} %copy.32), channel_id=1, replica_groups=mesh['frames'=2,'row'=4,'col'=4] {'col'}, dimensions={0}, use_global_device_ids=true | all-gather | bytes 655360 | tf_op jit(solution)/shard_map/all_gather | solution.py:95
  28.0 1.3 %collective-permute-start.2 = (bf16[16,544]{1,0:T(8,128)(2,1)S(1)}, bf16[16,544]{1,0:T(8,128)(2,1)S(1)}, u32[]{:S(2)}, u32[]{:S(2)}) collective-permute-start(bf16[16,544]{1,0:T(8,128)(2,1)S(1)} %get-tuple-element.134), channel_id=1, source_target_pairs={{0,4},{4,8},{8,12},{1,5},{5,9},{9,13},{2,6},{6,10},{10,14},{3,7},{... | collective-permute-start | bytes 52232 | tf_op jit(solution)/shard_map/ppermute | solution.py:19
  29.3 1.3 %collective-permute-start.3 = (bf16[16,544]{1,0:T(8,128)(2,1)S(1)}, bf16[16,544]{1,0:T(8,128)(2,1)S(1)}, u32[]{:S(2)}, u32[]{:S(2)}) collective-permute-start(bf16[16,544]{1,0:T(8,128)(2,1)S(1)} %get-tuple-element.135), channel_id=1, source_target_pairs={{4,0},{8,4},{12,8},{5,1},{9,5},{13,9},{6,2},{10,6},{14,10},{7,3},{... | collective-permute-start | bytes 52232 | tf_op jit(solution)/shard_map/ppermute | solution.py:20
  30.8 1.3 %copy.30 = bf16[12,2,160,128]{3,2,1,0:T(8,128)(2,1)} copy(bf16[12,2,160,128]{3,0,1,2:T(8,128)(2,1)S(1)} %fusion.29) | data formatting | bytes 1966080
  32.5 1.6 %collective-permute-done.3 = bf16[16,544]{1,0:T(8,128)(2,1)S(1)} collective-permute-done((bf16[16,544]{1,0:T(8,128)(2,1)S(1)}, bf16[16,544]{1,0:T(8,128)(2,1)S(1)}, u32[]{:S(2)}, u32[]{:S(2)}) %collective-permute-start.3) | collective-permute-done | bytes 17440 | tf_op jit(solution)/shard_map/ppermute | solution.py:20
  35.2 39.7 %while.13 = (s32[]{:T(128)}, f32[256,512]{1,0:T(8,128)S(1)}, f32[12]{0:T(128)S(1)}, bf16[12,2,160,128]{3,2,1,0:T(8,128)(2,1)}, bf16[12,2,160,128]{3,2,1,0:T(8,12...) while((s32[]{:T(128)}, f32[256,512]{1,0:T(8,128)S(1)}, ...), condition=%wide.region_3.4_spmd.clone, body=%wide.region_1.3_spmd.clone.sunk | while | flops 180649984 | bytes 8913533 | solution.py:138
  35.9 1.3 %fusion.88 = f32[128,2,512]{2,0,1:T(8,128)S(1)} fusion(bf16[2,2,32,512]{3,2,1,0:T(8,128)(2,1)S(1)} %slice.94, bf16[2,2,128,512]{3,2,1,0:T(8,128)(2,1)S(1)} %slice.95, bf16[12,2,160,128]{3,2,1,0:T(8,128)(2,1)} %get-tuple-element.200, s32[]{:T(128)} %get-tuple-element.188), kind=kOutput, calls=%fused_computation.2.clone.1 | convolution fusion | flops 85590016 | bytes 1262080 | tf_op jit(solution)/shard_map/while/body/eval_jaxpr/pbiw,pij->pbjw/dot_general | solution.py:128
  37.1 0.6 dynamic_slice.36
  37.7 0.6 broadcast_multiply_fusion.2
  39.2 1.3 %fusion.88 = f32[128,2,512]{2,0,1:T(8,128)S(1)} fusion(bf16[2,2,32,512]{3,2,1,0:T(8,128)(2,1)S(1)} %slice.94, bf16[2,2,128,512]{3,2,1,0:T(8,128)(2,1)S(1)} %slice.95, bf16[12,2,160,128]{3,2,1,0:T(8,128)(2,1)} %get-tuple-element.200, s32[]{:T(128)} %get-tuple-element.188), kind=kOutput, calls=%fused_computation.2.clone.1 | convolution fusion | flops 85590016 | bytes 1262080 | tf_op jit(solution)/shard_map/while/body/eval_jaxpr/pbiw,pij->pbjw/dot_general | solution.py:128
  40.4 0.6 dynamic_slice.36
  41.0 0.6 broadcast_multiply_fusion.2
  42.5 1.3 %fusion.88 = f32[128,2,512]{2,0,1:T(8,128)S(1)} fusion(bf16[2,2,32,512]{3,2,1,0:T(8,128)(2,1)S(1)} %slice.94, bf16[2,2,128,512]{3,2,1,0:T(8,128)(2,1)S(1)} %slice.95, bf16[12,2,160,128]{3,2,1,0:T(8,128)(2,1)} %get-tuple-element.200, s32[]{:T(128)} %get-tuple-element.188), kind=kOutput, calls=%fused_computation.2.clone.1 | convolution fusion | flops 85590016 | bytes 1262080 | tf_op jit(solution)/shard_map/while/body/eval_jaxpr/pbiw,pij->pbjw/dot_general | solution.py:128
  43.8 0.6 dynamic_slice.36
  44.3 0.6 broadcast_multiply_fusion.2
  45.8 1.3 %fusion.88 = f32[128,2,512]{2,0,1:T(8,128)S(1)} fusion(bf16[2,2,32,512]{3,2,1,0:T(8,128)(2,1)S(1)} %slice.94, bf16[2,2,128,512]{3,2,1,0:T(8,128)(2,1)S(1)} %slice.95, bf16[12,2,160,128]{3,2,1,0:T(8,128)(2,1)} %get-tuple-element.200, s32[]{:T(128)} %get-tuple-element.188), kind=kOutput, calls=%fused_computation.2.clone.1 | convolution fusion | flops 85590016 | bytes 1262080 | tf_op jit(solution)/shard_map/while/body/eval_jaxpr/pbiw,pij->pbjw/dot_general | solution.py:128
  47.7 0.6 broadcast_multiply_fusion.2
  49.1 1.3 %fusion.88 = f32[128,2,512]{2,0,1:T(8,128)S(1)} fusion(bf16[2,2,32,512]{3,2,1,0:T(8,128)(2,1)S(1)} %slice.94, bf16[2,2,128,512]{3,2,1,0:T(8,128)(2,1)S(1)} %slice.95, bf16[12,2,160,128]{3,2,1,0:T(8,128)(2,1)} %get-tuple-element.200, s32[]{:T(128)} %get-tuple-element.188), kind=kOutput, calls=%fused_computation.2.clone.1 | convolution fusion | flops 85590016 | bytes 1262080 | tf_op jit(solution)/shard_map/while/body/eval_jaxpr/pbiw,pij->pbjw/dot_general | solution.py:128
  51.0 0.6 broadcast_multiply_fusion.2
  52.4 1.3 %fusion.88 = f32[128,2,512]{2,0,1:T(8,128)S(1)} fusion(bf16[2,2,32,512]{3,2,1,0:T(8,128)(2,1)S(1)} %slice.94, bf16[2,2,128,512]{3,2,1,0:T(8,128)(2,1)S(1)} %slice.95, bf16[12,2,160,128]{3,2,1,0:T(8,128)(2,1)} %get-tuple-element.200, s32[]{:T(128)} %get-tuple-element.188), kind=kOutput, calls=%fused_computation.2.clone.1 | convolution fusion | flops 85590016 | bytes 1262080 | tf_op jit(solution)/shard_map/while/body/eval_jaxpr/pbiw,pij->pbjw/dot_general | solution.py:128
  54.3 0.6 broadcast_multiply_fusion.2
  55.7 1.3 %fusion.88 = f32[128,2,512]{2,0,1:T(8,128)S(1)} fusion(bf16[2,2,32,512]{3,2,1,0:T(8,128)(2,1)S(1)} %slice.94, bf16[2,2,128,512]{3,2,1,0:T(8,128)(2,1)S(1)} %slice.95, bf16[12,2,160,128]{3,2,1,0:T(8,128)(2,1)} %get-tuple-element.200, s32[]{:T(128)} %get-tuple-element.188), kind=kOutput, calls=%fused_computation.2.clone.1 | convolution fusion | flops 85590016 | bytes 1262080 | tf_op jit(solution)/shard_map/while/body/eval_jaxpr/pbiw,pij->pbjw/dot_general | solution.py:128
  57.6 0.6 broadcast_multiply_fusion.2
  59.0 1.3 %fusion.88 = f32[128,2,512]{2,0,1:T(8,128)S(1)} fusion(bf16[2,2,32,512]{3,2,1,0:T(8,128)(2,1)S(1)} %slice.94, bf16[2,2,128,512]{3,2,1,0:T(8,128)(2,1)S(1)} %slice.95, bf16[12,2,160,128]{3,2,1,0:T(8,128)(2,1)} %get-tuple-element.200, s32[]{:T(128)} %get-tuple-element.188), kind=kOutput, calls=%fused_computation.2.clone.1 | convolution fusion | flops 85590016 | bytes 1262080 | tf_op jit(solution)/shard_map/while/body/eval_jaxpr/pbiw,pij->pbjw/dot_general | solution.py:128
  60.9 0.6 broadcast_multiply_fusion.2
  62.3 1.3 %fusion.88 = f32[128,2,512]{2,0,1:T(8,128)S(1)} fusion(bf16[2,2,32,512]{3,2,1,0:T(8,128)(2,1)S(1)} %slice.94, bf16[2,2,128,512]{3,2,1,0:T(8,128)(2,1)S(1)} %slice.95, bf16[12,2,160,128]{3,2,1,0:T(8,128)(2,1)} %get-tuple-element.200, s32[]{:T(128)} %get-tuple-element.188), kind=kOutput, calls=%fused_computation.2.clone.1 | convolution fusion | flops 85590016 | bytes 1262080 | tf_op jit(solution)/shard_map/while/body/eval_jaxpr/pbiw,pij->pbjw/dot_general | solution.py:128
  64.2 0.6 broadcast_multiply_fusion.2
  65.6 1.3 %fusion.88 = f32[128,2,512]{2,0,1:T(8,128)S(1)} fusion(bf16[2,2,32,512]{3,2,1,0:T(8,128)(2,1)S(1)} %slice.94, bf16[2,2,128,512]{3,2,1,0:T(8,128)(2,1)S(1)} %slice.95, bf16[12,2,160,128]{3,2,1,0:T(8,128)(2,1)} %get-tuple-element.200, s32[]{:T(128)} %get-tuple-element.188), kind=kOutput, calls=%fused_computation.2.clone.1 | convolution fusion | flops 85590016 | bytes 1262080 | tf_op jit(solution)/shard_map/while/body/eval_jaxpr/pbiw,pij->pbjw/dot_general | solution.py:128
  67.5 0.6 broadcast_multiply_fusion.2
  68.9 1.3 %fusion.88 = f32[128,2,512]{2,0,1:T(8,128)S(1)} fusion(bf16[2,2,32,512]{3,2,1,0:T(8,128)(2,1)S(1)} %slice.94, bf16[2,2,128,512]{3,2,1,0:T(8,128)(2,1)S(1)} %slice.95, bf16[12,2,160,128]{3,2,1,0:T(8,128)(2,1)} %get-tuple-element.200, s32[]{:T(128)} %get-tuple-element.188), kind=kOutput, calls=%fused_computation.2.clone.1 | convolution fusion | flops 85590016 | bytes 1262080 | tf_op jit(solution)/shard_map/while/body/eval_jaxpr/pbiw,pij->pbjw/dot_general | solution.py:128
  70.8 0.6 broadcast_multiply_fusion.2
  72.3 1.3 %fusion.88 = f32[128,2,512]{2,0,1:T(8,128)S(1)} fusion(bf16[2,2,32,512]{3,2,1,0:T(8,128)(2,1)S(1)} %slice.94, bf16[2,2,128,512]{3,2,1,0:T(8,128)(2,1)S(1)} %slice.95, bf16[12,2,160,128]{3,2,1,0:T(8,128)(2,1)} %get-tuple-element.200, s32[]{:T(128)} %get-tuple-element.188), kind=kOutput, calls=%fused_computation.2.clone.1 | convolution fusion | flops 85590016 | bytes 1262080 | tf_op jit(solution)/shard_map/while/body/eval_jaxpr/pbiw,pij->pbjw/dot_general | solution.py:128
  74.1 0.6 broadcast_multiply_fusion.2
  75.0 4.4 %collective-permute-start.4 = (bf16[8,512]{1,0:T(8,128)(2,1)S(1)}, bf16[8,512]{1,0:T(8,128)(2,1)S(1)}, u32[]{:S(2)}, u32[]{:S(2)}) collective-permute-start(bf16[8,512]{1,0:T(8,128)(2,1)S(1)} %get-tuple-element.138), channel_id=1, source_target_pairs={{0,4},{4,8},{8,12},{1,5},{5,9},{9,13},{2,6},{6,10},{10,14},{3,7},{... | collective-permute-start | bytes 24584 | tf_op jit(solution)/shard_map/ppermute | solution.py:19
  79.5 1.3 %collective-permute-start.5 = (bf16[8,512]{1,0:T(8,128)(2,1)S(1)}, bf16[8,512]{1,0:T(8,128)(2,1)S(1)}, u32[]{:S(2)}, u32[]{:S(2)}) collective-permute-start(bf16[8,512]{1,0:T(8,128)(2,1)S(1)} %get-tuple-element.139), channel_id=1, source_target_pairs={{4,0},{8,4},{12,8},{5,1},{9,5},{13,9},{6,2},{10,6},{14,10},{7,3},{... | collective-permute-start | bytes 24584 | tf_op jit(solution)/shard_map/ppermute | solution.py:20
  80.9 0.6 fusion.66
  81.6 1.0 %collective-permute-done.5 = bf16[8,512]{1,0:T(8,128)(2,1)S(1)} collective-permute-done((bf16[8,512]{1,0:T(8,128)(2,1)S(1)}, bf16[8,512]{1,0:T(8,128)(2,1)S(1)}, u32[]{:S(2)}, u32[]{:S(2)}) %collective-permute-start.5) | collective-permute-done | bytes 8224 | tf_op jit(solution)/shard_map/ppermute | solution.py:20
  82.6 3.9 %collective-permute-start.6 = (bf16[272,8]{1,0:T(8,128)(2,1)S(1)}, bf16[272,8]{1,0:T(8,128)(2,1)S(1)}, u32[]{:S(2)}, u32[]{:S(2)}) collective-permute-start(bf16[272,8]{1,0:T(8,128)(2,1)S(1)} %get-tuple-element.136), channel_id=1, source_target_pairs={{0,1},{1,2},{2,3},{4,5},{5,6},{6,7},{8,9},{9,10},{10,11},{12,13},{... | collective-permute-start | bytes 13064 | tf_op jit(solution)/shard_map/ppermute | solution.py:19
  86.5 1.3 %collective-permute-start.7 = (bf16[272,8]{1,0:T(8,128)(2,1)S(1)}, bf16[272,8]{1,0:T(8,128)(2,1)S(1)}, u32[]{:S(2)}, u32[]{:S(2)}) collective-permute-start(bf16[272,8]{1,0:T(8,128)(2,1)S(1)} %get-tuple-element.137), channel_id=1, source_target_pairs={{1,0},{2,1},{3,2},{5,4},{6,5},{7,6},{9,8},{10,9},{11,10},{13,12},{... | collective-permute-start | bytes 13064 | tf_op jit(solution)/shard_map/ppermute | solution.py:20
  87.8 1.2 %fusion.18 = f32[1,144,128]{2,0,1:T(1,128)S(1)} fusion(pred[144,128,17]{1,0,2:T(8,128)(4,1)S(1)} %iota_compare_fusion.1, f32[]{:T(128)} %fusion.66), kind=kOutput, calls=%fused_computation.22 | convolution fusion | flops 3760230 | bytes 387076 | tf_op jit(solution)/shard_map/...t,ijt->...ij/dot_general | solution.py:32
  89.0 3.7 %collective-permute-done.7 = bf16[272,8]{1,0:T(8,128)(2,1)S(1)} collective-permute-done((bf16[272,8]{1,0:T(8,128)(2,1)S(1)}, bf16[272,8]{1,0:T(8,128)(2,1)S(1)}, u32[]{:S(2)}, u32[]{:S(2)}) %collective-permute-start.7) | collective-permute-done | bytes 4384 | tf_op jit(solution)/shard_map/ppermute | solution.py:20
  93.3 2.3 %fusion.32 = f32[272,4,128]{2,0,1:T(8,128)S(1)} fusion(f32[144,128,1]{1,0,2:T(8,128)S(1)} %bitcast.115, f32[272,4,16]{0,2,1:T(8,128)S(1)} %slice.85, f32[272,4,128]{0,2,1:T(8,128)S(1)} %slice.84), kind=kOutput, calls=%fused_computation.30 | convolution fusion | flops 240804864 | bytes 1257472 | tf_op jit(solution)/shard_map/rbi,ij->rbj/dot_general | solution.py:70
  96.4 1.4 %fusion.41 = f32[128,2,512]{2,0,1:T(8,128)} fusion(f32[144,128,1]{1,0,2:T(8,128)S(1)} %bitcast.116, f32[2,16,512]{2,1,0:T(8,128)S(1)} %slice.87, f32[2,128,512]{2,1,0:T(8,128)S(1)} %slice.72), kind=kOutput, calls=%fused_computation.40 | convolution fusion | flops 226639872 | bytes 1187840 | tf_op jit(solution)/shard_map/biw,ij->bjw/dot_general | solution.py:74
  (126 shorter events, 18.4 us)
Async XLA Ops:
  0.0 8.9 %copy-start.2 = (bf16[12,2,33]{2,1,0:T(2,128)(2,1)S(1)}, bf16[12,2,33]{2,1,0:T(2,128)(2,1)}, u32[]{:S(2)}) copy-start(bf16[12,2,33]{2,1,0:T(2,128)(2,1)} %param.11) | copy-start | bytes 4756
  1.2 26.7 %collective-permute-start = (bf16[256,16]{1,0:T(8,128)(2,1)S(1)}, bf16[256,16]{1,0:T(8,128)(2,1)S(1)}, u32[]{:S(2)}, u32[]{:S(2)}) collective-permute-start(bf16[256,16]{1,0:T(8,128)(2,1)S(1)} %get-tuple-element.140), channel_id=1, source_target_pairs={{0,1},{1,2},{2,3},{4,5},{5,6},{6,7},{8,9},{9,10},{10,11},{12,13},{... | collective-permute-start | bytes 24584 | tf_op jit(solution)/shard_map/ppermute | solution.py:19
  6.1 21.8 %collective-permute-start.1 = (bf16[256,16]{1,0:T(8,128)(2,1)S(1)}, bf16[256,16]{1,0:T(8,128)(2,1)S(1)}, u32[]{:S(2)}, u32[]{:S(2)}) collective-permute-start(bf16[256,16]{1,0:T(8,128)(2,1)S(1)} %get-tuple-element.141), channel_id=1, source_target_pairs={{1,0},{2,1},{3,2},{5,4},{6,5},{7,6},{9,8},{10,9},{11,10},{13,12},{... | collective-permute-start | bytes 24584 | tf_op jit(solution)/shard_map/ppermute | solution.py:20
  8.9 1.9 %copy-start.1 = (bf16[8,64,128]{2,1,0:T(8,128)(2,1)S(1)}, bf16[8,64,128]{2,1,0:T(8,128)(2,1)}, u32[]{:S(2)}) copy-start(bf16[8,64,128]{2,1,0:T(8,128)(2,1)} %param.14) | copy-start | bytes 393220
  8.9 2.6 %copy-start.3 = (s32[1,1,8]{2,1,0:T(1,128)S(1)}, s32[1,1,8]{2,1,0:T(1,128)}, u32[]{:S(2)}) copy-start(s32[1,1,8]{2,1,0:T(1,128)} %param.15) | copy-start | bytes 100
  8.9 2.6 %copy-start.4 = (s32[1,1,8]{2,1,0:T(1,128)S(1)}, s32[1,1,8]{2,1,0:T(1,128)}, u32[]{:S(2)}) copy-start(s32[1,1,8]{2,1,0:T(1,128)} %param.16) | copy-start | bytes 100
  28.0 4.5 %collective-permute-start.2 = (bf16[16,544]{1,0:T(8,128)(2,1)S(1)}, bf16[16,544]{1,0:T(8,128)(2,1)S(1)}, u32[]{:S(2)}, u32[]{:S(2)}) collective-permute-start(bf16[16,544]{1,0:T(8,128)(2,1)S(1)} %get-tuple-element.134), channel_id=1, source_target_pairs={{0,4},{4,8},{8,12},{1,5},{5,9},{9,13},{2,6},{6,10},{10,14},{3,7},{... | collective-permute-start | bytes 52232 | tf_op jit(solution)/shard_map/ppermute | solution.py:19
  29.3 4.8 %collective-permute-start.3 = (bf16[16,544]{1,0:T(8,128)(2,1)S(1)}, bf16[16,544]{1,0:T(8,128)(2,1)S(1)}, u32[]{:S(2)}, u32[]{:S(2)}) collective-permute-start(bf16[16,544]{1,0:T(8,128)(2,1)S(1)} %get-tuple-element.135), channel_id=1, source_target_pairs={{4,0},{8,4},{12,8},{5,1},{9,5},{13,9},{6,2},{10,6},{14,10},{7,3},{... | collective-permute-start | bytes 52232 | tf_op jit(solution)/shard_map/ppermute | solution.py:20
  30.8 1.3 %copy-start = (bf16[12,2,160,128]{3,0,1,2:T(8,128)(2,1)S(1)}, bf16[12,2,160,128]{3,0,1,2:T(8,128)(2,1)}, u32[]{:S(2)}) copy-start(bf16[12,2,160,128]{3,0,1,2:T(8,128)(2,1)} %fusion.26) | copy-start | bytes 2949124
  34.5 0.7 copy-start.5
  75.0 6.5 %collective-permute-start.4 = (bf16[8,512]{1,0:T(8,128)(2,1)S(1)}, bf16[8,512]{1,0:T(8,128)(2,1)S(1)}, u32[]{:S(2)}, u32[]{:S(2)}) collective-permute-start(bf16[8,512]{1,0:T(8,128)(2,1)S(1)} %get-tuple-element.138), channel_id=1, source_target_pairs={{0,4},{4,8},{8,12},{1,5},{5,9},{9,13},{2,6},{6,10},{10,14},{3,7},{... | collective-permute-start | bytes 24584 | tf_op jit(solution)/shard_map/ppermute | solution.py:19
  79.5 3.1 %collective-permute-start.5 = (bf16[8,512]{1,0:T(8,128)(2,1)S(1)}, bf16[8,512]{1,0:T(8,128)(2,1)S(1)}, u32[]{:S(2)}, u32[]{:S(2)}) collective-permute-start(bf16[8,512]{1,0:T(8,128)(2,1)S(1)} %get-tuple-element.139), channel_id=1, source_target_pairs={{4,0},{8,4},{12,8},{5,1},{9,5},{13,9},{6,2},{10,6},{14,10},{7,3},{... | collective-permute-start | bytes 24584 | tf_op jit(solution)/shard_map/ppermute | solution.py:20
  82.6 6.4 %collective-permute-start.6 = (bf16[272,8]{1,0:T(8,128)(2,1)S(1)}, bf16[272,8]{1,0:T(8,128)(2,1)S(1)}, u32[]{:S(2)}, u32[]{:S(2)}) collective-permute-start(bf16[272,8]{1,0:T(8,128)(2,1)S(1)} %get-tuple-element.136), channel_id=1, source_target_pairs={{0,1},{1,2},{2,3},{4,5},{5,6},{6,7},{8,9},{9,10},{10,11},{12,13},{... | collective-permute-start | bytes 13064 | tf_op jit(solution)/shard_map/ppermute | solution.py:19
  86.5 6.2 %collective-permute-start.7 = (bf16[272,8]{1,0:T(8,128)(2,1)S(1)}, bf16[272,8]{1,0:T(8,128)(2,1)S(1)}, u32[]{:S(2)}, u32[]{:S(2)}) collective-permute-start(bf16[272,8]{1,0:T(8,128)(2,1)S(1)} %get-tuple-element.137), channel_id=1, source_target_pairs={{1,0},{2,1},{3,2},{5,4},{6,5},{7,6},{9,8},{10,9},{11,10},{13,12},{... | collective-permute-start | bytes 13064 | tf_op jit(solution)/shard_map/ppermute | solution.py:20
where the time goes:
time: 99.3 us; the launch traced here: 97.8 us
  matrix products  28.8 us (29%)
  starting transfers between devices  19.7 us (20%)
  blocking collectives  16.1 us (16%)
  local copies, waits for them, and re-layouts  13.4 us (13%)
  other arithmetic  11.7 us (12%)
  waiting for transfers between devices  6.27 us (6%)
    all_gather x1, blocking collectives, place_cells(): shard_cells = lax.all_gather(library, 'col', axis=0, tiled=True)  16.1 us
    dot_general x12, matrix products, kernel_step(): jnp.einsum('pbiw,pij->pbjw', windows_rows(pass_one, half_width), second_m...  15.3 us
    ppermute x4, starting transfers between devices, extended_2(): before = lax.ppermute(last, axis, up)  14.5 us
    mul x12, other arithmetic, kernel_step(): return (running + weight * jnp.sum(pass_two * pass_two, axis=0), None)  7.17 us
    dynamic_slice x12, local copies, waits for them, and re-layouts, on_device(): lax.scan(kernel_step, start_total, (first_mats, second_mats, kernel_weigh...  7.1 us
    ppermute x4, waiting for transfers between devices, extended_2(): after = lax.ppermute(initial, axis, down)  6.26 us
    ppermute x4, starting transfers between devices, extended_2(): after = lax.ppermute(initial, axis, down)  5.17 us
    dot_general x12, matrix products, kernel_step(): jnp.einsum('rbi,pij->prbj', tall_windows, first_mat, preferred_element_ty...  4.83 us
  transfers between devices with their start and end apart: 8, of which 3 were waited for; matrix products, arithmetic and copies ran while one was open for 8% of the time, Pallas kernels for 0%

commit v1 on v0

v1 whole, which is shorter than its diff:
```python
import functools
import math

import jax
import jax.numpy as jnp
from jax import lax
from jax.experimental import pallas as pl
from jax.experimental.pallas import tpu as pltpu
from jax.sharding import PartitionSpec as P

BLUR = 8
SIGMA = 4.0
GAUSS_SUM = sum(math.exp(-(t * t) / (2.0 * SIGMA * SIGMA)) for t in range(-BLUR, BLUR + 1))
MESH = pl.DeviceIdType.MESH
F32 = jnp.float32
BF16 = jnp.bfloat16
LANES = 128
AROUND = [(i, j) for i in (-1, 0, 1) for j in (-1, 0, 1)]
HERE = 4
RIM_ROWS = 32


def gauss_band(shape, in_dim):
    step = lax.broadcasted_iota(jnp.int32, shape, in_dim) - lax.broadcasted_iota(
        jnp.int32, shape, 1 - in_dim
    )
    lag = step.astype(F32) - BLUR
    value = jnp.exp(-lag * lag / (2.0 * SIGMA * SIGMA)) * (1.0 / GAUSS_SUM)
    value = jnp.where((step >= 0) & (step <= 2 * BLUR), value, 0.0)
    high = value.astype(BF16)
    return high, (value - high.astype(F32)).astype(BF16)


def dot(a, b):
    return jnp.dot(a, b, preferred_element_type=F32)


def kernel(
    half,
    n_row,
    n_col,
    mask_ref,
    across_ref,
    down_ref,
    weights_ref,
    library_ref,
    ids_ref,
    slots_ref,
    count_ref,
    out_ref,
    own,
    up_down,
    left_right,
    corners,
    mask_ext,
    tap_rows,
    down_mats,
    across_mats,
    first,
    total,
    high,
    low,
    cells,
    table,
    tables,
    tables_s,
    mask_send,
    mask_recv,
    table_send,
    table_recv,
    cell_send,
    cell_recv,
    table_sem,
):
    rows, cols = mask_ref.shape
    kernels = across_ref.shape[0]
    taps = 2 * half + 1
    rim = half + BLUR
    wide = own.shape[1]
    out_rows = rows + 2 * BLUR
    blocks = cols // LANES
    n_cells, cell_rows, _ = library_ref.shape
    slot_rows = rows // cell_rows
    row, col = lax.axis_index("row"), lax.axis_index("col")

    def exists(dr, dc):
        ok = None
        for here, step, count in ((row, dr, n_row), (col, dc, n_col)):
            if step < 0:
                one = here >= -step
            elif step > 0:
                one = here < count - step
            else:
                continue
            ok = one if ok is None else ok & one
        return ok

    def device(dr, dc):
        return {"row": row + dr, "col": col + dc}

    peers = [(0, j) for j in range(-(n_col - 1), n_col) if j != 0]
    near = [o for o in AROUND if o != (0, 0)]
    partners = near + [o for o in peers if abs(o[1]) > 1]

    barrier = pltpu.get_barrier_semaphore()
    for o in partners:

        @pl.when(exists(*o))
        def _():
            pl.semaphore_signal(barrier, inc=1, device_id=device(*o), device_id_type=MESH)

    pixels = mask_ref[...].astype(F32)
    pixels = jnp.concatenate([pixels, jnp.zeros((rows, wide - cols), F32)], axis=1)
    own[...] = pltpu.roll(pixels, rim, 1).astype(BF16)
    entries = ids_ref.shape[-1]
    at_slot = lax.broadcasted_iota(jnp.int32, table.shape, 0)
    value = jnp.zeros(table.shape, jnp.int32)
    for n in range(entries):
        entry = jnp.where(n < count_ref[0, 0], ids_ref[0, 0, n] + 1, 0)
        value = value + jnp.where(at_slot == slots_ref[0, 0, n], entry, 0)
    table[...] = value

    pl.semaphore_wait(barrier, sum(jnp.where(exists(*o), 1, 0) for o in partners))

    def mask_copy(dr, dc):
        row_part = {-1: pl.ds(0, RIM_ROWS), 0: pl.ds(0, rows), 1: pl.ds(rows - RIM_ROWS, RIM_ROWS)}
        col_part = {-1: pl.ds(0, LANES), 0: pl.ds(0, wide), 1: pl.ds(cols, LANES)}
        slot = AROUND.index((-dr, -dc))
        if dc == 0:
            target = up_down.at[(1 - dr) // 2]
        elif dr == 0:
            target = left_right.at[(1 - dc) // 2]
        else:
            target = corners.at[(1 - dr) // 2 * 2 + (1 - dc) // 2]
        return pltpu.make_async_remote_copy(
            src_ref=own.at[row_part[dr], col_part[dc]],
            dst_ref=target,
            send_sem=mask_send.at[slot],
            recv_sem=mask_recv.at[slot],
            device_id=device(dr, dc),
            device_id_type=MESH,
        )

    def table_copy(dr, dc):
        slot = AROUND.index((-dr, -dc))
        return pltpu.make_async_remote_copy(
            src_ref=table,
            dst_ref=tables.at[slot],
            send_sem=table_send.at[slot],
            recv_sem=table_recv.at[slot],
            device_id=device(dr, dc),
            device_id_type=MESH,
        )

    def cell_copy(dc, owner):
        return pltpu.make_async_remote_copy(
            src_ref=library_ref,
            dst_ref=cells.at[pl.ds(owner * n_cells, n_cells)],
            send_sem=cell_send.at[dc + n_col],
            recv_sem=cell_recv.at[dc + n_col],
            device_id=device(0, dc),
            device_id_type=MESH,
        )

    for o in near:

        @pl.when(exists(*o))
        def _():
            mask_copy(*o).start()

    for o in near:

        @pl.when(exists(*o))
        def _():
            table_copy(*o).start()

    for _, dc in sorted(peers, key=lambda o: abs(o[1])):

        @pl.when(exists(0, dc))
        def _():
            cell_copy(dc, col).start()

    tap_rows[...] = jnp.zeros_like(tap_rows)
    for k in range(kernels):
        tap_rows[0, 2 * k : 2 * k + 2, :taps] = down_ref[k].astype(F32)
        tap_rows[1, 2 * k : 2 * k + 2, :taps] = across_ref[k].astype(F32)
    pick = lax.broadcasted_iota(jnp.int32, (LANES, 2 * LANES), 0)
    lane = lax.broadcasted_iota(jnp.int32, (LANES, 2 * LANES), 1)
    shift = RIM_ROWS - rim
    forward = (lane == pick + shift).astype(BF16)
    backward = ((lane + pick) % (2 * LANES) == 0).astype(BF16)
    base_down = dot(tap_rows[0, :, :LANES].astype(BF16), forward)
    base_across = dot(tap_rows[1, :, :LANES].astype(BF16), backward)
    tap_rows[0] = base_down
    tap_rows[1] = base_across
    band_rows = down_mats.shape[1]

    def build(i, carry):
        one = jnp.broadcast_to(tap_rows[0, pl.ds(i, 1), :], (band_rows, 2 * LANES))
        down_mats[i] = pltpu.roll(one, 0, 1, stride=1, stride_axis=0).astype(BF16)
        one = jnp.broadcast_to(tap_rows[1, pl.ds(i, 1), :], (2 * LANES, 2 * LANES))
        across_mats[i] = pltpu.roll(one, 0, 1, stride=1, stride_axis=0).astype(BF16)
        return carry

    lax.fori_loop(0, 2 * kernels, build, 0)

    total[...] = jnp.zeros_like(total)
    mask_ext[rows + 2 * RIM_ROWS :, :] = jnp.zeros_like(mask_ext[rows + 2 * RIM_ROWS :, :])
    cells[pl.ds(col * n_cells, n_cells)] = library_ref[...]
    tables[HERE] = table[...]

    for o in near:
        slot = AROUND.index(o)

        @pl.when(exists(*o))
        def _():
            table_copy(-o[0], -o[1]).wait_recv()

        @pl.when(jnp.logical_not(exists(*o)))
        def _():
            tables[slot] = jnp.zeros(tables.shape[1:], jnp.int32)

    to_scalar = pltpu.make_async_copy(tables, tables_s, table_sem)
    to_scalar.start()

    for o in near:
        dr, dc = o

        @pl.when(exists(*o))
        def _():
            mask_copy(-dr, -dc).wait_recv()

        @pl.when(jnp.logical_not(exists(*o)))
        def _():
            if dc == 0:
                up_down[(1 + dr) // 2] = jnp.zeros(up_down.shape[1:], BF16)
            elif dr == 0:
                left_right[(1 + dc) // 2] = jnp.zeros(left_right.shape[1:], BF16)
            else:
                corners[(1 + dr) // 2 * 2 + (1 + dc) // 2] = jnp.zeros(corners.shape[1:], BF16)

    def extend(start, body, left, right):
        count = body.shape[0]
        part = pl.ds(start, count)
        near_edge = lax.broadcasted_iota(jnp.int32, (count, LANES), 1) < 2 * rim
        mask_ext[part, 0:LANES] = body[:, 0:LANES] + left
        mask_ext[part, LANES:cols] = body[:, LANES:cols]
        mask_ext[part, cols:wide] = body[:, cols:wide] + jnp.where(
            near_edge, right.astype(F32), 0.0
        ).astype(BF16)

    extend(0, up_down[0], corners[0], corners[1])
    extend(RIM_ROWS, own[...], left_right[0], left_right[1])
    extend(RIM_ROWS + rows, up_down[1], corners[2], corners[3])

    rest = out_rows - band_rows

    def down_pass(k, carry):
        lhs = down_mats[pl.ds(2 * k, 2)].reshape(2 * band_rows, 2 * LANES)
        got = dot(lhs, mask_ext[0 : 2 * LANES, :]).astype(BF16)
        first[2 * k, 0:band_rows] = got[:band_rows]
        first[2 * k + 1, 0:band_rows] = got[band_rows:]
        got = dot(lhs, mask_ext[band_rows : band_rows + 2 * LANES, :]).astype(BF16)
        first[2 * k, band_rows:] = got[:rest]
        first[2 * k + 1, band_rows:] = got[band_rows : band_rows + rest]
        return carry

    lax.fori_loop(0, kernels, down_pass, 0)

    def across_pass(k, carry):
        weight = weights_ref[k]
        for w in range(blocks):
            start = w * LANES
            stop = start + LANES if w < blocks - 1 else wide
            sums = None
            for p in range(2):
                got = dot(
                    first[2 * k + p, :, start : start + 2 * LANES],
                    across_mats[2 * k + p, :, : stop - start],
                )
                sums = got * got if sums is None else sums + got * got
            total[:, start:stop] = total[:, start:stop] + weight * sums
        return carry

    lax.fori_loop(0, kernels, across_pass, 0)

    for _, dc in peers:

        @pl.when(exists(0, dc))
        def _():
            cell_copy(-dc, col + dc).wait_recv()

    to_scalar.wait()

    def image(where, slot, part):
        entry = tables_s[where, slot, 0]
        scale = jnp.where(entry > 0, 1.0, 0.0)
        index = jnp.minimum(jnp.maximum(entry - 1, 0), cells.shape[0] - 1)
        return cells[index, part, :].astype(F32) * scale

    def place(start, dr, slot_row, part, keep):
        middle = AROUND.index((dr, 0))
        pieces = [image(middle, slot_row * blocks + b, part) for b in range(blocks)]
        before = image(middle - 1, slot_row * blocks + blocks - 1, part)
        after = image(middle + 1, slot_row * blocks, part)
        first_half = lax.broadcasted_iota(jnp.int32, before.shape, 1) < LANES // 2
        pieces.append(jnp.where(first_half, after, before))
        band = pltpu.roll(jnp.concatenate(pieces, axis=1), BLUR, 1)[keep]
        total[start : start + band.shape[0], :] = total[start : start + band.shape[0], :] + band

    place(0, -1, slot_rows - 1, pl.ds(cell_rows - 16, 16), slice(8, 16))
    for a in range(slot_rows):
        place(BLUR + a * cell_rows, 0, a, pl.ds(0, cell_rows), slice(0, cell_rows))
    place(BLUR + rows, 1, 0, pl.ds(0, 16), slice(0, 8))

    row_from = jnp.where(row == 0, BLUR, 0)
    row_to = jnp.where(row == n_row - 1, BLUR + rows, out_rows)
    col_from = jnp.where(col == 0, BLUR, 0)
    col_to = jnp.where(col == n_col - 1, BLUR + cols, cols + 2 * BLUR)
    at_row = lax.broadcasted_iota(jnp.int32, (out_rows, wide), 0)
    at_col = lax.broadcasted_iota(jnp.int32, (out_rows, wide), 1)
    inside = (at_row >= row_from) & (at_row < row_to) & (at_col >= col_from) & (at_col < col_to)
    value = jnp.where(inside, total[...], 0.0)
    top = value.astype(BF16)
    high[...] = top
    low[...] = (value - top.astype(F32)).astype(BF16)

    g_high, g_low = gauss_band((2 * LANES, LANES), 0)
    for w in range(blocks):
        here = slice(w * LANES, (w + 2) * LANES)
        got = dot(high[:, here], g_high) + dot(low[:, here], g_high) + dot(high[:, here], g_low)
        total[:, w * LANES : (w + 1) * LANES] = got
    value = total[:, :cols]
    top = value.astype(BF16)
    high[:, :cols] = top
    low[:, :cols] = (value - top.astype(F32)).astype(BF16)
    g_high, g_low = gauss_band((LANES, LANES + 2 * BLUR), 1)
    for r in range(rows // LANES):
        here = slice(r * LANES, (r + 1) * LANES + 2 * BLUR)
        out_ref[r * LANES : (r + 1) * LANES, :] = (
            dot(g_high, high[here, :cols])
            + dot(g_high, low[here, :cols])
            + dot(g_low, high[here, :cols])
        )

    for o in near:

        @pl.when(exists(*o))
        def _():
            mask_copy(*o).wait_send()
            table_copy(*o).wait_send()

    for _, dc in peers:

        @pl.when(exists(0, dc))
        def _():
            cell_copy(dc, col).wait_send()


def on_device(n_row, n_col, *args):
    mask_pixels, across_taps, _, _, library, cell_ids, _, _ = args
    rows, cols = mask_pixels.shape
    kernels = across_taps.shape[0]
    half = (across_taps.shape[-1] - 1) // 2
    wide = cols + LANES
    out_rows = rows + 2 * BLUR
    n_cells, cell_rows, cell_cols = library.shape
    n_slots = (rows // cell_rows) * (cols // cell_cols)
    band_rows = 144
    vmem = pl.BlockSpec(memory_space=pltpu.VMEM)
    smem = pl.BlockSpec(memory_space=pltpu.SMEM)
    dma = pltpu.SemaphoreType.DMA
    return pl.pallas_call(
        functools.partial(kernel, half, n_row, n_col),
        out_shape=jax.ShapeDtypeStruct((rows, cols), F32),
        in_specs=[vmem, vmem, vmem, smem, vmem, smem, smem, smem],
        out_specs=vmem,
        scratch_shapes=[
            pltpu.VMEM((rows, wide), BF16),
            pltpu.VMEM((2, RIM_ROWS, wide), BF16),
            pltpu.VMEM((2, rows, LANES), BF16),
            pltpu.VMEM((4, RIM_ROWS, LANES), BF16),
            pltpu.VMEM((band_rows + 2 * LANES, wide), BF16),
            pltpu.VMEM((2, 2 * kernels, 2 * LANES), F32),
            pltpu.VMEM((2 * kernels, band_rows, 2 * LANES), BF16),
            pltpu.VMEM((2 * kernels, 2 * LANES, 2 * LANES), BF16),
            pltpu.VMEM((2 * kernels, out_rows, wide), BF16),
            pltpu.VMEM((out_rows, wide), F32),
            pltpu.VMEM((out_rows, wide), BF16),
            pltpu.VMEM((out_rows, wide), BF16),
            pltpu.VMEM((n_cells * n_col, cell_rows, cell_cols), BF16),
            pltpu.VMEM((n_slots, LANES), jnp.int32),
            pltpu.VMEM((len(AROUND), n_slots, LANES), jnp.int32),
            pltpu.SMEM((len(AROUND), n_slots, LANES), jnp.int32),
            dma((len(AROUND),)),
            dma((len(AROUND),)),
            dma((len(AROUND),)),
            dma((len(AROUND),)),
            dma((2 * n_col,)),
            dma((2 * n_col,)),
            dma,
        ],
        compiler_params=pltpu.CompilerParams(
            collective_id=0, has_side_effects=True, vmem_limit_bytes=48 * 2**20
        ),
    )(*args)


def solution(mesh):
    placed = (
        P(("frames", "row"), "col"),
        P(),
        P(),
        P(),
        P("col", None, None),
        P(("frames", "row"), "col", None),
        P(("frames", "row"), "col", None),
        P(("frames", "row"), "col"),
    )
    return jax.shard_map(
        functools.partial(on_device, mesh.shape["row"], mesh.shape["col"]),
        mesh=mesh,
        in_specs=placed,
        out_specs=P(("frames", "row"), "col"),
        check_vma=False,
    )
```

time: 99.3 us -> 27.4 us (0.28); the launches traced: 97.8 us -> 27.1 us
  matrix products: 28.8 us -> 0 us
  Pallas kernels: 0 us -> 22.2 us
  starting transfers between devices: 19.7 us -> 0 us
  blocking collectives: 16.1 us -> 0 us
  other arithmetic: 11.7 us -> 0 us
  local copies, waits for them, and re-layouts: 13.4 us -> 4.13 us
  waiting for transfers between devices: 6.27 us -> 0 us
    dot_general x31 -> x0, matrix products: 28.8 us -> none  [the longest x12 15.3 us: kernel_step(): jnp.einsum('pbiw,pij->pbjw', windows_rows(pass_one, half_width), second_m...]
    pallas_call x0 -> x1, Pallas kernels: none -> 22.2 us  [on_device(): pl.pallas_call(functools.partial(kernel, half, n_row, n_col), out_shape=j...]
    ppermute x8 -> x0, starting transfers between devices: 19.7 us -> none  [the longest x4 14.5 us: extended_2(): before = lax.ppermute(last, axis, up)]
    all_gather x1 -> x0, blocking collectives: 16.1 us -> none  [place_cells(): shard_cells = lax.all_gather(library, 'col', axis=0, tiled=True)]
    mul x12 -> x0, other arithmetic: 7.17 us -> none  [kernel_step(): return (running + weight * jnp.sum(pass_two * pass_two, axis=0), None)]
    dynamic_slice x12 -> x0, local copies, waits for them, and re-layouts: 7.1 us -> none  [on_device(): lax.scan(kernel_step, start_total, (first_mats, second_mats, kernel_weigh...]
    ppermute x8 -> x0, waiting for transfers between devices: 6.27 us -> none  [the longest x4 6.26 us: extended_2(): after = lax.ppermute(initial, axis, down)]
    add x12 -> x0, other arithmetic: 1.89 us -> none  [kernel_step(): return (running + weight * jnp.sum(pass_two * pass_two, axis=0), None)]
  transfers between devices with their start and end apart: 8 -> 0, of which waited for: 3 -> 0; matrix products, arithmetic and copies ran while one was open for 8% -> 0% of each run, Pallas kernels for 0% -> 0%
where the time goes in v1:
time: 27.4 us; the launch traced here: 27.1 us
  Pallas kernels  22.2 us (81%)
  local copies, waits for them, and re-layouts  4.13 us (15%)
  between operations  0.74 us (3%)
    pallas_call x1, Pallas kernels, on_device(): pl.pallas_call(functools.partial(kernel, half, n_row, n_col), out_shape=j...  22.2 us
    unnamed x15, local copies, waits for them, and re-layouts  4.13 us

profile of v1, /device:TPU:0, one launch (start us, length us, event | category | flops | bytes accessed | tf_op | source)
XLA Modules:
  0.0 27.1 jit_solution(6514943719408212767)
XLA Ops:
  0.0 0.0 copy-start.6
  0.0 0.0 copy-start.5
  0.0 0.0 copy-start.4
  0.7 0.0 copy-done.6
  0.7 0.0 copy-done.5
  0.7 0.0 copy-done.4
  0.7 0.0 copy-start
  0.7 1.0 %copy-done = s32[256,512]{1,0:T(8,128)S(1)} copy-done((s32[256,512]{1,0:T(8,128)S(1)}, s32[256,512]{1,0:T(8,128)}, u32[]{:S(2)}) %copy-start) | copy-done | bytes 524312
  1.8 0.0 copy-start.1
  1.8 0.9 %copy-done.1 = bf16[8,64,128]{2,1,0:T(8,128)(2,1)S(1)} copy-done((bf16[8,64,128]{2,1,0:T(8,128)(2,1)S(1)}, bf16[8,64,128]{2,1,0:T(8,128)(2,1)}, u32[]{:S(2)}) %copy-start.1) | copy-done | bytes 131096
  2.7 0.0 copy-start.2
  2.7 0.7 %copy-done.2 = bf16[12,2,33]{2,1,0:T(2,128)(2,1)S(1)} copy-done((bf16[12,2,33]{2,1,0:T(2,128)(2,1)S(1)}, bf16[12,2,33]{2,1,0:T(2,128)(2,1)}, u32[]{:S(2)}) %copy-start.2) | copy-done | bytes 1608
  3.4 0.0 copy-start.3
  3.4 0.7 %copy-done.3 = bf16[12,2,33]{2,1,0:T(2,128)(2,1)S(1)} copy-done((bf16[12,2,33]{2,1,0:T(2,128)(2,1)S(1)}, bf16[12,2,33]{2,1,0:T(2,128)(2,1)}, u32[]{:S(2)}) %copy-start.3) | copy-done | bytes 1608
  4.1 22.2 %shard_map.82 = f32[256,512]{1,0:T(8,128)S(1)} custom-call(s32[256,512]{1,0:T(8,128)S(1)} %copy-done, bf16[12,2,33]{2,1,0:T(2,128)(2,1)S(1)} %copy-done.2, bf16[12,2,33]{2,1,0:T(2,128)(2,1)S(1)} %copy-done.3, f32[12]{0:T(128)S(1)} %copy-done.4, bf16[8,64,128]{2,1,0:T(8,128)(2,1)S(1)} %copy-done.1, s32[1,1,8]{2,1,0:T(1,128)S(1)} %copy-done.5, ...), custom_call_target="tpu_custom_call" | custom-call | tf_op jit(solution)/shard_map/pallas_call | solution.py:373
  26.3 0.8 %copy.11 = f32[256,512]{1,0:T(8,128)} copy(f32[256,512]{1,0:T(8,128)S(1)} %shard_map.82) | data formatting | bytes 1048576
Async XLA Ops:
  0.0 0.7 %copy-start.6 = (s32[1,1,8]{2,1,0:T(1,128)S(1)}, s32[1,1,8]{2,1,0:T(1,128)}, u32[]{:S(2)}) copy-start(s32[1,1,8]{2,1,0:T(1,128)} %slots_ref.1) | copy-start | bytes 100
  0.0 0.7 %copy-start.5 = (s32[1,1,8]{2,1,0:T(1,128)S(1)}, s32[1,1,8]{2,1,0:T(1,128)}, u32[]{:S(2)}) copy-start(s32[1,1,8]{2,1,0:T(1,128)} %ids_ref.1) | copy-start | bytes 100
  0.0 0.7 %copy-start.4 = (f32[12]{0:T(128)S(1)}, f32[12]{0:T(128)}, u32[]{:S(2)}) copy-start(f32[12]{0:T(128)} %weights_ref.1) | copy-start | bytes 148
  0.7 1.0 %copy-start = (s32[256,512]{1,0:T(8,128)S(1)}, s32[256,512]{1,0:T(8,128)}, u32[]{:S(2)}) copy-start(s32[256,512]{1,0:T(8,128)} %mask_ref.1) | copy-start | bytes 1572868
  1.8 0.9 %copy-start.1 = (bf16[8,64,128]{2,1,0:T(8,128)(2,1)S(1)}, bf16[8,64,128]{2,1,0:T(8,128)(2,1)}, u32[]{:S(2)}) copy-start(bf16[8,64,128]{2,1,0:T(8,128)(2,1)} %library_ref.1) | copy-start | bytes 393220
  2.7 0.7 %copy-start.2 = (bf16[12,2,33]{2,1,0:T(2,128)(2,1)S(1)}, bf16[12,2,33]{2,1,0:T(2,128)(2,1)}, u32[]{:S(2)}) copy-start(bf16[12,2,33]{2,1,0:T(2,128)(2,1)} %across_ref.1) | copy-start | bytes 4756
  3.4 0.7 %copy-start.3 = (bf16[12,2,33]{2,1,0:T(2,128)(2,1)S(1)}, bf16[12,2,33]{2,1,0:T(2,128)(2,1)}, u32[]{:S(2)}) copy-start(bf16[12,2,33]{2,1,0:T(2,128)(2,1)} %down_ref.1) | copy-start | bytes 4756

commit v2 on v1

--- a/solution.py
+++ b/solution.py
@@ -39,9 +39,9 @@
     half,
     n_row,
     n_col,
-    mask_ref,
-    across_ref,
-    down_ref,
+    mask_hbm,
+    across_hbm,
+    down_hbm,
     weights_ref,
     library_ref,
     ids_ref,
@@ -71,7 +71,21 @@
     cell_send,
     cell_recv,
     table_sem,
+    mask_ref,
+    across_ref,
+    down_ref,
+    fetch_sems,
+    pass_send,
+    pass_recv,
 ):
+    fetches = [
+        pltpu.make_async_copy(source, target, fetch_sems.at[i])
+        for i, (source, target) in enumerate(
+            ((mask_hbm, mask_ref), (down_hbm, down_ref), (across_hbm, across_ref))
+        )
+    ]
+    for fetch in fetches:
+        fetch.start()
     rows, cols = mask_ref.shape
     kernels = across_ref.shape[0]
     taps = 2 * half + 1
@@ -109,6 +123,7 @@
         def _():
             pl.semaphore_signal(barrier, inc=1, device_id=device(*o), device_id_type=MESH)
 
+    fetches[0].wait()
     pixels = mask_ref[...].astype(F32)
     pixels = jnp.concatenate([pixels, jnp.zeros((rows, wide - cols), F32)], axis=1)
     own[...] = pltpu.roll(pixels, rim, 1).astype(BF16)
@@ -152,10 +167,24 @@
             device_id_type=MESH,
         )
 
+    core = lax.rem(row, 2)
+    half_cells = n_cells // 2
+
+    def pass_on(dc, part):
+        block = cells.at[pl.ds((col + dc) * n_cells + part * half_cells, half_cells)]
+        return pltpu.make_async_remote_copy(
+            src_ref=block,
+            dst_ref=block,
+            send_sem=pass_send.at[dc + n_col],
+            recv_sem=pass_recv.at[dc + n_col],
+            device_id=device(1 - 2 * core, 0),
+            device_id_type=MESH,
+        )
+
     def cell_copy(dc, owner):
         return pltpu.make_async_remote_copy(
-            src_ref=library_ref,
-            dst_ref=cells.at[pl.ds(owner * n_cells, n_cells)],
+            src_ref=library_ref.at[pl.ds(core * half_cells, half_cells)],
+            dst_ref=cells.at[pl.ds(owner * n_cells + core * half_cells, half_cells)],
             send_sem=cell_send.at[dc + n_col],
             recv_sem=cell_recv.at[dc + n_col],
             device_id=device(0, dc),
@@ -180,6 +209,13 @@
         def _():
             cell_copy(dc, col).start()
 
+    own_cells = pltpu.make_async_copy(
+        library_ref, cells.at[pl.ds(col * n_cells, n_cells)], fetch_sems.at[3]
+    )
+    own_cells.start()
+
+    fetches[1].wait()
+    fetches[2].wait()
     tap_rows[...] = jnp.zeros_like(tap_rows)
     for k in range(kernels):
         tap_rows[0, 2 * k : 2 * k + 2, :taps] = down_ref[k].astype(F32)
@@ -206,7 +242,7 @@
 
     total[...] = jnp.zeros_like(total)
     mask_ext[rows + 2 * RIM_ROWS :, :] = jnp.zeros_like(mask_ext[rows + 2 * RIM_ROWS :, :])
-    cells[pl.ds(col * n_cells, n_cells)] = library_ref[...]
+    own_cells.wait()
     tables[HERE] = table[...]
 
     for o in near:
@@ -266,6 +302,13 @@
         return carry
 
     lax.fori_loop(0, kernels, down_pass, 0)
+
+    for _, dc in peers:
+
+        @pl.when(exists(0, dc))
+        def _():
+            cell_copy(-dc, col + dc).wait_recv()
+            pass_on(dc, core).start()
 
     def across_pass(k, carry):
         weight = weights_ref[k]
@@ -288,7 +331,7 @@
 
         @pl.when(exists(0, dc))
         def _():
-            cell_copy(-dc, col + dc).wait_recv()
+            pass_on(dc, 1 - core).wait_recv()
 
     to_scalar.wait()
 
@@ -355,6 +398,7 @@
         @pl.when(exists(0, dc))
         def _():
             cell_copy(dc, col).wait_send()
+            pass_on(dc, core).wait_send()
 
 
 def on_device(n_row, n_col, *args):
@@ -368,12 +412,13 @@
     n_slots = (rows // cell_rows) * (cols // cell_cols)
     band_rows = 144
     vmem = pl.BlockSpec(memory_space=pltpu.VMEM)
+    hbm = pl.BlockSpec(memory_space=pltpu.HBM)
     smem = pl.BlockSpec(memory_space=pltpu.SMEM)
     dma = pltpu.SemaphoreType.DMA
     return pl.pallas_call(
         functools.partial(kernel, half, n_row, n_col),
         out_shape=jax.ShapeDtypeStruct((rows, cols), F32),
-        in_specs=[vmem, vmem, vmem, smem, vmem, smem, smem, smem],
+        in_specs=[hbm, hbm, hbm, smem, hbm, smem, smem, smem],
         out_specs=vmem,
         scratch_shapes=[
             pltpu.VMEM((rows, wide), BF16),
@@ -399,9 +444,15 @@
             dma((2 * n_col,)),
             dma((2 * n_col,)),
             dma,
+            pltpu.VMEM(mask_pixels.shape, mask_pixels.dtype),
+            pltpu.VMEM(across_taps.shape, across_taps.dtype),
+            pltpu.VMEM(across_taps.shape, across_taps.dtype),
+            dma((4,)),
+            dma((2 * n_col,)),
+            dma((2 * n_col,)),
         ],
         compiler_params=pltpu.CompilerParams(
-            collective_id=0, has_side_effects=True, vmem_limit_bytes=48 * 2**20
+            collective_id=0, has_side_effects=True, vmem_limit_bytes=62 * 2**20
         ),
     )(*args)
 

time: 27.4 us -> 26.1 us (0.953)
  local copies, waits for them, and re-layouts: 4.13 us -> 1.87 us
  Pallas kernels: 22.2 us -> 23.4 us
    unnamed x15 -> x1, local copies, waits for them, and re-layouts: 4.13 us -> 1.87 us
    pallas_call x1, Pallas kernels: 22.2 us -> 23.4 us  [on_device(): pl.pallas_call(functools.partial(kernel, half, n_row, n_col), out_shape=j...]
where the time goes in v2:
time: 26.1 us; the launch traced here: 25.9 us
  Pallas kernels  23.4 us (90%)
  local copies, waits for them, and re-layouts  1.87 us (7%)
  between operations  0.66 us (3%)
    pallas_call x1, Pallas kernels, on_device(): pl.pallas_call(functools.partial(kernel, half, n_row, n_col), out_shape=j...  23.4 us
    unnamed x1, local copies, waits for them, and re-layouts  1.87 us

profile of v2, /device:TPU:0, one launch (start us, length us, event | category | flops | bytes accessed | tf_op | source)
XLA Modules:
  0.0 25.9 jit_solution(13559667241866374406)
XLA Ops:
  0.7 23.4 %shard_map.82 = f32[256,512]{1,0:T(8,128)} custom-call(s32[256,512]{1,0:T(8,128)} %mask_hbm.1, bf16[12,2,33]{2,1,0:T(2,128)(2,1)} %across_hbm.1, bf16[12,2,33]{2,1,0:T(2,128)(2,1)} %down_hbm.1, f32[12]{0:T(128)} %weights_ref.1, bf16[8,64,128]{2,1,0:T(8,128)(2,1)} %library_ref.1, s32[1,1,8]{2,1,0:T(1,128)} %ids_ref.1, s32[1,1,8]{2,1,0:T(1,128)} %slots_ref.1, ...), custom_call_target="tpu_custom_call" | custom-call | tf_op jit(solution)/shard_map/pallas_call | solution.py:418
  24.1 1.9 %copy.11 = f32[256,512]{1,0:T(8,128)} copy(f32[256,512]{1,0:T(8,128)} %shard_map.82) | data formatting | bytes 1048576

commit v3 on v2

--- a/solution.py
+++ b/solution.py
@@ -238,7 +238,7 @@
         across_mats[i] = pltpu.roll(one, 0, 1, stride=1, stride_axis=0).astype(BF16)
         return carry
 
-    lax.fori_loop(0, 2 * kernels, build, 0)
+    lax.fori_loop(0, 2 * kernels, build, 0, unroll=4)
 
     total[...] = jnp.zeros_like(total)
     mask_ext[rows + 2 * RIM_ROWS :, :] = jnp.zeros_like(mask_ext[rows + 2 * RIM_ROWS :, :])
@@ -301,7 +301,7 @@
         first[2 * k + 1, band_rows:] = got[band_rows : band_rows + rest]
         return carry
 
-    lax.fori_loop(0, kernels, down_pass, 0)
+    lax.fori_loop(0, kernels, down_pass, 0, unroll=2)
 
     for _, dc in peers:
 
@@ -325,7 +325,7 @@
             total[:, start:stop] = total[:, start:stop] + weight * sums
         return carry
 
-    lax.fori_loop(0, kernels, across_pass, 0)
+    lax.fori_loop(0, kernels, across_pass, 0, unroll=3)
 
     for _, dc in peers:
 

time: 26.1 us -> 24.9 us (0.954)
  Pallas kernels: 23.4 us -> 22.1 us
    pallas_call x1, Pallas kernels: 23.4 us -> 22.1 us  [on_device(): pl.pallas_call(functools.partial(kernel, half, n_row, n_col), out_shape=j...]
where the time goes in v3:
time: 24.9 us; the launch traced here: 24.7 us
  Pallas kernels  22.1 us (89%)
  local copies, waits for them, and re-layouts  1.87 us (8%)
  between operations  0.66 us (3%)
    pallas_call x1, Pallas kernels, on_device(): pl.pallas_call(functools.partial(kernel, half, n_row, n_col), out_shape=j...  22.1 us
    unnamed x1, local copies, waits for them, and re-layouts  1.87 us

profile of v3, /device:TPU:0, one launch (start us, length us, event | category | flops | bytes accessed | tf_op | source)
XLA Modules:
  0.0 24.7 jit_solution(980983524496395064)
XLA Ops:
  0.7 22.1 %shard_map.82 = f32[256,512]{1,0:T(8,128)} custom-call(s32[256,512]{1,0:T(8,128)} %mask_hbm.1, bf16[12,2,33]{2,1,0:T(2,128)(2,1)} %across_hbm.1, bf16[12,2,33]{2,1,0:T(2,128)(2,1)} %down_hbm.1, f32[12]{0:T(128)} %weights_ref.1, bf16[8,64,128]{2,1,0:T(8,128)(2,1)} %library_ref.1, s32[1,1,8]{2,1,0:T(1,128)} %ids_ref.1, s32[1,1,8]{2,1,0:T(1,128)} %slots_ref.1, ...), custom_call_target="tpu_custom_call" | custom-call | tf_op jit(solution)/shard_map/pallas_call | solution.py:418
  22.8 1.9 %copy.11 = f32[256,512]{1,0:T(8,128)} copy(f32[256,512]{1,0:T(8,128)} %shard_map.82) | data formatting | bytes 1048576

commit v4 on v3

--- a/solution.py
+++ b/solution.py
@@ -303,13 +303,6 @@
 
     lax.fori_loop(0, kernels, down_pass, 0, unroll=2)
 
-    for _, dc in peers:
-
-        @pl.when(exists(0, dc))
-        def _():
-            cell_copy(-dc, col + dc).wait_recv()
-            pass_on(dc, core).start()
-
     def across_pass(k, carry):
         weight = weights_ref[k]
         for w in range(blocks):
@@ -325,7 +318,17 @@
             total[:, start:stop] = total[:, start:stop] + weight * sums
         return carry
 
-    lax.fori_loop(0, kernels, across_pass, 0, unroll=3)
+    early = kernels * 3 // 4
+    lax.fori_loop(0, early, across_pass, 0, unroll=3)
+
+    for _, dc in peers:
+
+        @pl.when(exists(0, dc))
+        def _():
+            cell_copy(-dc, col + dc).wait_recv()
+            pass_on(dc, core).start()
+
+    lax.fori_loop(early, kernels, across_pass, 0, unroll=3)
 
     for _, dc in peers:
 

time: 24.9 us -> 23.7 us (0.952)
  Pallas kernels: 22.1 us -> 20.9 us
    pallas_call x1, Pallas kernels: 22.1 us -> 20.9 us  [on_device(): pl.pallas_call(functools.partial(kernel, half, n_row, n_col), out_shape=j...]
where the time goes in v4:
time: 23.7 us; the launch traced here: 23.5 us
  Pallas kernels  20.9 us (88%)
  local copies, waits for them, and re-layouts  1.87 us (8%)
  between operations  0.66 us (3%)
    pallas_call x1, Pallas kernels, on_device(): pl.pallas_call(functools.partial(kernel, half, n_row, n_col), out_shape=j...  20.9 us
    unnamed x1, local copies, waits for them, and re-layouts  1.87 us

profile of v4, /device:TPU:0, one launch (start us, length us, event | category | flops | bytes accessed | tf_op | source)
XLA Modules:
  0.0 23.5 jit_solution(2428450614516896871)
XLA Ops:
  0.7 20.9 %shard_map.82 = f32[256,512]{1,0:T(8,128)} custom-call(s32[256,512]{1,0:T(8,128)} %mask_hbm.1, bf16[12,2,33]{2,1,0:T(2,128)(2,1)} %across_hbm.1, bf16[12,2,33]{2,1,0:T(2,128)(2,1)} %down_hbm.1, f32[12]{0:T(128)} %weights_ref.1, bf16[8,64,128]{2,1,0:T(8,128)(2,1)} %library_ref.1, s32[1,1,8]{2,1,0:T(1,128)} %ids_ref.1, s32[1,1,8]{2,1,0:T(1,128)} %slots_ref.1, ...), custom_call_target="tpu_custom_call" | custom-call | tf_op jit(solution)/shard_map/pallas_call | solution.py:421
  21.6 1.9 %copy.11 = f32[256,512]{1,0:T(8,128)} copy(f32[256,512]{1,0:T(8,128)} %shard_map.82) | data formatting | bytes 1048576
